TPU v7x, 128 devices: a whole 4x4x4 slice. The times are simulated.
128 devices in a mesh: dp: 32 (over y, x, z_hi), expert: 4 (over z_lo, core).
Axes of the slice: x: 4, y: 4, z: 4 (z_hi: 2, z_lo: 2; z = z_hi * 2 + z_lo), core: 2. Of those that a mesh axis runs over, the one named last changes fastest.
Arguments:
- patches: bfloat16 [512, 256, 1152], P(('dp', 'expert')), may hold values from -6 to 6
- norm_gain: bfloat16 [1152], replicated, may hold values from 0.25 to 1.75
- router: bfloat16 [1152, 128], replicated, may hold values from -0.1875 to 0.1875
- expert_in: bfloat16 [128, 1152, 4304], P(('dp', 'expert')), may hold values from -0.1875 to 0.1875
- expert_out: bfloat16 [128, 4304, 1152], P(('dp', 'expert')), may hold values from -0.09375 to 0.09375
- post_gain: bfloat16 [1152], replicated, may hold values from 0.25 to 1.75
- key_query: bfloat16 [16, 1152], replicated, may hold values from -0.1875 to 0.1875
- value_proj: bfloat16 [1152, 1152], replicated, may hold values from -0.1875 to 0.1875
- out_proj: bfloat16 [1152, 1152], replicated, may hold values from -0.1875 to 0.1875
- text_embed: bfloat16 [512, 1152], P(('dp', 'expert')), may hold values from -6 to 6
- inverse_heat_exponent: float32 [1], replicated, may hold values from 1.8 to 2.6
- score_intercept: float32 [1], replicated, may hold values from -5 to -1.5
Outputs:
- pooled: float32 [512, 1152], P(('dp', 'expert'))
- pooled_grad: float32 [512, 1152], P(('dp', 'expert'))
- text_grad: float32 [512, 1152], P(('dp', 'expert'))
All inputs are finite; a program needn't handle non-finite values.
Results may differ from a plain program's by a relative error of at most 0.015.
Values may be sent and summed in bfloat16 or wider, within the bound.
A program may use at most 128 MiB of HBM per device.

v0:
```python
import jax
import jax.numpy as jnp
from jax import lax
from jax.sharding import PartitionSpec as P


def layer_norm(inputs_f32, gain_vector):
    center = jnp.mean(inputs_f32, axis=-1, keepdims=True)
    shifted = inputs_f32 - center
    spread = jnp.mean(shifted * shifted, axis=-1, keepdims=True)
    return shifted * lax.rsqrt(spread + 1e-06) * gain_vector.astype(jnp.float32)


def run_experts(expert_rows, expert_in, expert_out):
    hidden = jax.nn.gelu(
        jnp.einsum("nkd,kdf->nkf", expert_rows, expert_in, preferred_element_type=jnp.float32),
        approximate=True,
    ).astype(jnp.bfloat16)
    return jnp.einsum(
        "nkf,kfd->nkd", hidden, expert_out, preferred_element_type=jnp.float32
    ).astype(jnp.bfloat16)


def body(
    patches,
    norm_gain,
    router,
    expert_in,
    expert_out,
    post_gain,
    key_query,
    value_proj,
    out_proj,
    text_embed,
    inverse_heat_exponent,
    score_intercept,
):
    images, patch_count, model_width = patches.shape
    dp_count = lax.axis_size("dp")
    group_size = lax.axis_size("expert")
    normed = layer_norm(patches.astype(jnp.float32), norm_gain).astype(jnp.bfloat16)
    logits = jnp.einsum("ipd,ds->ips", normed, router, preferred_element_type=jnp.float32)
    slot_peak = jnp.max(logits, axis=1, keepdims=True)
    weighted = jnp.exp(logits - slot_peak)
    dispatch = (weighted / jnp.sum(weighted, axis=1, keepdims=True)).astype(jnp.bfloat16)
    combine = jax.nn.softmax(logits, axis=2).astype(jnp.bfloat16)
    slot_in = jnp.einsum(
        "ips,ipd->isd", dispatch, normed, preferred_element_type=jnp.float32
    ).astype(jnp.bfloat16)
    expert_rows = lax.all_to_all(slot_in, ("dp", "expert"), split_axis=1, concat_axis=0, tiled=True)
    answers = run_experts(expert_rows, expert_in, expert_out)
    slot_out = lax.all_to_all(answers, ("dp", "expert"), split_axis=0, concat_axis=1, tiled=True)
    mixed_tokens = patches.astype(jnp.float32) + jnp.einsum(
        "ips,isd->ipd", combine, slot_out, preferred_element_type=jnp.float32
    )
    pool_in = layer_norm(mixed_tokens, post_gain).astype(jnp.bfloat16)
    scores = jnp.einsum("ipd,hd->iph", pool_in, key_query, preferred_element_type=jnp.float32)
    head_peak = jnp.max(scores, axis=1, keepdims=True)
    attend = jnp.exp(scores - head_peak)
    head_mass = jnp.sum(attend, axis=1)
    head_sum = jnp.einsum(
        "iph,ipd->ihd", attend.astype(jnp.bfloat16), pool_in, preferred_element_type=jnp.float32
    )
    headed = (head_sum / head_mass[:, :, None]).astype(jnp.bfloat16)
    head_count = headed.shape[1]
    head_width = value_proj.shape[1] // head_count
    value_heads = value_proj.reshape(model_width, head_count, head_width)
    values = jnp.einsum(
        "ihd,dhe->ihe", headed, value_heads, preferred_element_type=jnp.float32
    ).astype(jnp.bfloat16)
    pooled = jnp.dot(
        values.reshape(images, head_count * head_width),
        out_proj,
        preferred_element_type=jnp.float32,
    )
    loss_rows = pooled.shape[0]
    inverse_heat_multiplier = jnp.exp(inverse_heat_exponent[0])
    target_sign_term = score_intercept[0]
    img_norm = jnp.sqrt(jnp.sum(pooled * pooled, axis=1, keepdims=True) + 1e-06)
    picture_direction_matrix = pooled / img_norm
    pair_total = loss_rows * dp_count * group_size
    first_row = (lax.axis_index("dp") * group_size + lax.axis_index("expert")) * loss_rows
    row_ids = first_row + jnp.arange(loss_rows, dtype=jnp.int32)
    text_piece = lax.all_gather(text_embed, ("dp", "expert"), axis=0, tiled=True)
    text_f32 = text_piece.astype(jnp.float32)
    text_norm = jnp.sqrt(jnp.sum(text_f32 * text_f32, axis=1, keepdims=True) + 1e-06)
    unit_text_rows = text_f32 / text_norm
    angular_agreement = jnp.dot(
        picture_direction_matrix, unit_text_rows.T, precision=lax.Precision.HIGHEST
    )
    couple_score_matrix = inverse_heat_multiplier * angular_agreement + target_sign_term
    col_ids = jnp.arange(text_piece.shape[0], dtype=jnp.int32)
    labels = jnp.where(row_ids[:, None] == col_ids[None, :], 1.0, -1.0).astype(jnp.float32)
    pairwise_factor = -labels * jax.nn.sigmoid(-labels * couple_score_matrix) / pair_total
    picture_derivative = inverse_heat_multiplier * jnp.dot(
        pairwise_factor, unit_text_rows, precision=lax.Precision.HIGHEST
    )
    folded = (picture_derivative, pairwise_factor)
    picture_derivative = folded[0]
    own_text = text_embed.astype(jnp.float32)
    own_norm = jnp.sqrt(jnp.sum(own_text * own_text, axis=1, keepdims=True) + 1e-06)
    own_unit = own_text / own_norm
    factor_table = folded[1]
    caption_direction_derivative = lax.psum_scatter(
        inverse_heat_multiplier
        * jnp.dot(factor_table.T, picture_direction_matrix, precision=lax.Precision.HIGHEST),
        ("dp", "expert"),
        scatter_dimension=0,
        tiled=True,
    )
    text_grad = (
        caption_direction_derivative
        - own_unit * jnp.sum(own_unit * caption_direction_derivative, axis=1, keepdims=True)
    ) / own_norm
    pooled_grad = (
        picture_derivative
        - picture_direction_matrix
        * jnp.sum(picture_direction_matrix * picture_derivative, axis=1, keepdims=True)
    ) / img_norm
    return (pooled, pooled_grad, text_grad)


def solution(mesh):
    placed = (
        P(("dp", "expert"), None, None),
        P(),
        P(),
        P(("dp", "expert"), None, None),
        P(("dp", "expert"), None, None),
        P(),
        P(),
        P(),
        P(),
        P(("dp", "expert"), None),
        P(),
        P(),
    )
    return jax.shard_map(
        body,
        mesh=mesh,
        in_specs=placed,
        out_specs=(P(("dp", "expert"), None), P(("dp", "expert"), None), P(("dp", "expert"), None)),
        check_vma=False,
    )
```

profile of v0, /device:TPU:1, one launch (start us, length us, event | category | flops | bytes accessed | tf_op | source)
XLA Modules:
  0.0 337.9 jit_solution(7707206005912924579)
XLA Ops:
  7.2 0.0 copy-start
  7.2 0.0 copy-start.2
  7.2 0.0 copy-start.6
  7.2 2.2 convert_reduce_fusion
  9.4 0.3 copy-done.2
  9.7 0.8 fusion.22
  10.5 1.0 fusion.33
  11.5 0.1 fusion.69
  11.6 3.8 %convolution_convert_fusion = bf16[4,128,1152]{2,1,0:T(8,128)(2,1)} fusion(bf16[4,256,1152]{2,1,0:T(8,128)(2,1)} %param.12, f32[1152]{0:T(1024)S(1)} %convert_element_type.59, f32[4,256]{1,0:T(4,128)S(1)} %add_rsqrt_fusion.1, f32[4,256]{1,0:T(4,128)S(1)} %broadcast_multiply_fusion.1, f32[4,128]{1,0:T(4,128)S(1)} %fusion.69, f32[4,256,128]{2,1,0:T(8,128)S(1)} %fusion.33), kind=kOutput, calls=%fused_computation.28 | convolution fusion | flops 308871936 | bytes 4078080 | tf_op jit(solution)/shard_map/ips,ipd->isd/dot_general | solution.py:47
  15.4 2.2 copy.30
  17.6 32.0 %all_to_all.33 = bf16[4,128,1152]{2,0,1:T(4,128)(2,1)} all-to-all(bf16[4,128,1152]{2,0,1:T(4,128)(2,1)S(1)} %copy.30), channel_id=1, replica_groups=mesh['dp'=32,'expert'=4] {'dp','expert'}, dimensions={1} | all-to-all | bytes 2359296 | tf_op jit(solution)/shard_map/all_to_all | solution.py:50
  49.6 3.5 %reshape.85 = bf16[512,1152]{1,0:T(8,128)(2,1)} reshape(bf16[128,4,1,1152]{3,1,0,2:T(4,128)(2,1)} %bitcast.74) | data formatting | bytes 2359296 | tf_op jit(solution)/shard_map/reshape.1
  53.1 31.8 %fusion.28 = bf16[512,1,1152]{2,0,1:T(8,128)(2,1)} fusion(bf16[1,4304,1152]{2,1,0:T(8,128)(2,1)} %param.16, bf16[512,1152]{1,0:T(8,128)(2,1)} %reshape.85, bf16[1,1152,4304]{1,2,0:T(8,128)(2,1)} %param.15), kind=kOutput, calls=%fused_computation.30 | convolution fusion | flops 10174832640 | bytes 22192128 | tf_op jit(solution)/shard_map/nkf,kfd->nkd/dot_general | solution.py:19
  84.9 0.5 broadcast.86
  85.4 3.5 %reduce.1 = bf16[512,1152]{1,0:T(8,128)(2,1)} reduce(bf16[512,1,1152]{2,0,1:T(8,128)(2,1)} %fusion.28, bf16[]{:T(256)} %broadcast.86), dimensions={1}, to_apply=%copy.31.reduce_sub_computation | reduce | bytes 2359298 | tf_op jit(solution)/shard_map/convert_element_type | solution.py:21
  88.8 3.7 %reshape.97 = bf16[128,2,2304]{2,1,0:T(2,128)(2,1)} reshape(bf16[512,1152]{1,0:T(8,128)(2,1)} %reduce.1) | data formatting | bytes 2359296
  92.5 5.6 %all-to-all-start.1 = ((bf16[128,2,2304]{2,1,0:T(2,128)(2,1)}), bf16[128,2,2304]{2,1,0:T(2,128)(2,1)}, u32[]{:S(2)}, u32[]{:S(2)}) async-start(bf16[128,2,2304]{2,1,0:T(2,128)(2,1)} %reshape.97), calls=%async_computation.1 | async-start | bytes 2359296 | tf_op jit(solution)/shard_map/all_to_all | solution.py:52
  98.2 0.0 all-gather.3.cloned.1.call-start
  98.2 0.7 all-gather.3.cloned.1.call-update
  98.9 0.0 all-reduce.3.cloned.1.call-start
  99.0 5.3 %copy.33 = bf16[1152,1152]{0,1:T(8,128)(2,1)} copy(bf16[1152,1152]{1,0:T(8,128)(2,1)} %param.19) | data formatting | bytes 5308416 | tf_op args[7]
  105.6 0.4 fusion.70
  105.9 12.6 %all-to-all-done.1 = bf16[128,2,2304]{2,1,0:T(2,128)(2,1)} async-done(((bf16[128,2,2304]{2,1,0:T(2,128)(2,1)}), bf16[128,2,2304]{2,1,0:T(2,128)(2,1)}, u32[]{:S(2)}, u32[]{:S(2)}) %all-to-all-start.1) | async-done | bytes 1179680 | tf_op jit(solution)/shard_map/all_to_all | solution.py:52
  118.6 8.0 %reshape.98 = bf16[512,1,1152]{2,1,0:T(2,128)(2,1)} reshape(bf16[128,2,2304]{2,1,0:T(2,128)(2,1)} %all-to-all-done.1) | data formatting | bytes 2359296
  126.6 9.2 %reduce = bf16[512,1152]{1,0:T(8,128)(2,1)} reduce(bf16[512,1,1152]{2,1,0:T(2,128)(2,1)} %reshape.98, bf16[]{:T(256)} %constant.48), dimensions={1}, to_apply=%all_to_all.27.reduce_sub_computation | reduce | bytes 2359298 | tf_op jit(solution)/shard_map/all_to_all | solution.py:52
  135.8 3.2 all_to_all.28
  139.0 6.2 %fusion.71 = (f32[4,256]{1,0:T(4,128)S(1)}, f32[4,256,1152]{2,1,0:T(8,128)}) fusion(bf16[128,4,1,1152]{3,1,0,2:T(4,128)(2,1)} %all_to_all.28, f32[4,256]{1,0:T(4,128)S(1)} %fusion.70, f32[4,256,128]{2,1,0:T(8,128)S(1)} %fusion.33, bf16[4,256,1152]{2,1,0:T(8,128)(2,1)} %param.12), kind=kOutput, calls=%fused_computation.92 | convolution fusion | flops 305922176 | bytes 8790016 | tf_op jit(solution)/shard_map/ips,isd->ipd/dot_general | solution.py:53
  145.3 3.1 multiply_reduce_fusion
  148.4 0.6 copy-done.1
  149.0 1.3 fusion.54
  150.3 0.2 fusion.72
  150.5 3.2 fusion.31
  153.7 2.6 fusion.43
  156.3 0.1 reshape.90
  156.5 0.6 multiply_reduce_fusion.4
  157.1 10.6 %all-gather.3.cloned.1.call-done = bf16[128,4,1152]{2,1,0:T(4,128)(2,1)} async-done(((bf16[1,4,1152]{2,1,0:T(4,128)(2,1)}), bf16[128,4,1152]{2,1,0:T(4,128)(2,1)}) %all-gather.3.cloned.1.call-update) | async-done | bytes 1179664 | tf_op jit(solution)/shard_map/all_gather | solution.py:84
  167.7 3.1 reshape.93
  170.8 1.9 multiply_reduce_fusion.1
  172.7 3.8 %fusion.51 = f32[4,512]{1,0:T(4,128)S(1)} fusion(f32[512,1152]{1,0:T(8,128)} %reshape.93, f32[512]{0:T(512)S(1)} %add_sqrt_fusion, f32[]{:T(128)} %bitcast.72, f32[]{:T(128)} %bitcast.19, s32[4]{0:T(128)S(1)} %iota_add_fusion, f32[4,1152]{1,0:T(4,128)S(1)} %get-tuple-element.6, f32[4]{0:T(128)S(1)} %add_sqrt_fusion.2), kind=kOutput, calls=%fused_computation.55 | convolution fusion | flops 28928512 | bytes 2388008 | tf_op jit(solution)/shard_map/dot_general | solution.py:88
  176.5 0.0 copy-start.4
  176.5 3.8 %convolution_multiply_fusion = f32[512,1152]{1,0:T(8,128)} fusion(f32[4,512]{1,0:T(4,128)S(1)} %fusion.51, f32[]{:T(128)} %bitcast.19, f32[4,1152]{1,0:T(4,128)S(1)} %get-tuple-element.6, f32[4]{0:T(128)S(1)} %add_sqrt_fusion.2), kind=kOutput, calls=%fused_computation.27 | convolution fusion | flops 28905984 | bytes 2385940 | tf_op jit(solution)/shard_map/dot_general | solution.py:106
  180.3 0.0 all-reduce.3.cloned.1.call-update
  180.3 0.1 fusion.61
  180.4 3.2 multiply_reduce_fusion.3
  183.6 0.7 subtract_divide_fusion.1
  184.3 144.1 %all-reduce.3.cloned.1.call-done = f32[512,1152]{1,0:T(8,128)} async-done(((f32[512,1152]{1,0:T(8,128)}), f32[512,1152]{1,0:T(8,128)}) %all-reduce.3.cloned.1.call-update) | async-done | bytes 2359312
  328.4 1.0 multiply_reduce_fusion.2
  329.4 1.5 subtract_divide_fusion
  (23 shorter events, 0.1 us)
Async XLA Ops:
  7.2 149.3 %copy-start = (bf16[1152,1152]{1,0:T(8,128)(2,1)S(1)}, bf16[1152,1152]{1,0:T(8,128)(2,1)}, u32[]{:S(2)}) copy-start(bf16[1152,1152]{1,0:T(8,128)(2,1)} %param.20) | copy-start | bytes 7962628
  7.2 2.5 copy-start.2
  7.2 3.3 copy-start.6
  7.2 3.3 copy-start.8
  88.8 10.1 %copy-start.7 = (bf16[1152]{0:T(1024)(128)(2,1)S(1)}, bf16[1152]{0:T(1024)(128)(2,1)}, u32[]{:S(2)}) copy-start(bf16[1152]{0:T(1024)(128)(2,1)} %param.17) | copy-start | bytes 6916
  92.5 26.0 %all-to-all-start.1 = ((bf16[128,2,2304]{2,1,0:T(2,128)(2,1)}), bf16[128,2,2304]{2,1,0:T(2,128)(2,1)}, u32[]{:S(2)}, u32[]{:S(2)}) async-start(bf16[128,2,2304]{2,1,0:T(2,128)(2,1)} %reshape.97), calls=%async_computation.1 | async-start | bytes 2359296 | tf_op jit(solution)/shard_map/all_to_all | solution.py:52
  98.2 69.5 %all-gather.3.cloned.1.call-start = ((), (), s32[]{:S(2)}) async-start(), calls=%async_computation.2 | async-start | bytes 1188864 | tf_op jit(solution)/shard_map/all_gather | solution.py:84
  98.9 229.5 %all-reduce.3.cloned.1.call-start = ((), (), s32[]{:S(2)}) async-start(), calls=%async_computation.3 | async-start | bytes 4718592
  139.0 9.3 %copy-start.5 = (bf16[16,1152]{1,0:T(8,128)(2,1)S(1)}, bf16[16,1152]{1,0:T(8,128)(2,1)}, u32[]{:S(2)}) copy-start(bf16[16,1152]{1,0:T(8,128)(2,1)} %param.18) | copy-start | bytes 110596
  145.3 3.8 %copy-start.1 = (f32[4,256,1152]{2,1,0:T(8,128)S(1)}, f32[4,256,1152]{2,1,0:T(8,128)}, u32[]{:S(2)}) copy-start(f32[4,256,1152]{2,1,0:T(8,128)} %get-tuple-element.4) | copy-start | bytes 14155780
  157.1 26.5 %copy-start.3 = (f32[4,1152]{1,0:T(4,128)}, f32[4,1152]{1,0:T(4,128)S(1)}, u32[]{:S(2)}) copy-start(f32[4,1152]{1,0:T(4,128)S(1)} %get-tuple-element.6) | copy-start | bytes 55300
  176.5 3.8 %copy-start.4 = (bf16[4,1152]{1,0:T(4,128)(2,1)S(1)}, bf16[4,1152]{1,0:T(4,128)(2,1)}, u32[]{:S(2)}) copy-start(bf16[4,1152]{1,0:T(4,128)(2,1)} %param.21) | copy-start | bytes 27652
Sparse Core Ops, SparseCore 0:
  101.8 65.8 all-gather.2
  180.4 147.9 all-reduce.2
where the time goes:
time: 343 us; the launch traced here: 338 us
  waiting for transfers between devices  168 us (49%)
  matrix products  61.2 us (18%)
  blocking collectives  32 us (9%)
  local copies, waits for them, and re-layouts  30.6 us (9%)
  other arithmetic  24.6 us (7%)
  between operations  15.8 us (5%)
  starting transfers between devices  5.7 us (2%)
    unnamed x3, waiting for transfers between devices  145 us
    all_to_all x1, blocking collectives, body(): lax.all_to_all(slot_in, ('dp', 'expert'), split_axis=1, concat_axis=0, ti...  32 us
    dot_general x1, matrix products, run_experts(): jnp.einsum('nkf,kfd->nkd', hidden, expert_out, preferred_element_type=jnp...  31.8 us
    unnamed x21, local copies, waits for them, and re-layouts  17.9 us
    all_to_all x1, waiting for transfers between devices, body(): lax.all_to_all(answers, ('dp', 'expert'), split_axis=0, concat_axis=1, ti...  12.6 us
    all_gather x1, waiting for transfers between devices, body(): lax.all_gather(text_embed, ('dp', 'expert'), axis=0, tiled=True)  10.6 us
    all_to_all x1, other arithmetic, body(): lax.all_to_all(answers, ('dp', 'expert'), split_axis=0, concat_axis=1, ti...  9.21 us
  transfers between devices with their start and end apart: 3, of which 3 were waited for; matrix products, arithmetic and copies ran while one was open for 13% of the time, Pallas kernels for 0%

commit v1 on v0

v1 whole, which is shorter than its diff:
```python
import functools

import jax
import jax.numpy as jnp
from jax import lax
from jax.experimental import pallas as pl
from jax.experimental.pallas import tpu as pltpu
from jax.sharding import PartitionSpec as P

MESH = pl.DeviceIdType.MESH
BF16, F32 = jnp.bfloat16, jnp.float32
BY_ROWS = (((1,), (1,)), ((), ()))
BY_COLUMNS = (((0,), (0,)), ((), ()))
EPS = 1e-6
GROUP = 2
STRIDE = 37
HIDDEN_STEP = 512
OUT_STEP = 384


def dot(a, b, dims=None):
    if dims is None:
        return jnp.dot(a, b, preferred_element_type=F32)
    return lax.dot_general(a, b, dims, preferred_element_type=F32)


def layer_norm(inputs, gain):
    center = jnp.mean(inputs, axis=1, keepdims=True)
    shifted = inputs - center
    spread = jnp.mean(shifted * shifted, axis=1, keepdims=True)
    return shifted * lax.rsqrt(spread + EPS) * gain


def norm_of(rows):
    return jnp.sqrt(jnp.sum(rows * rows, axis=1, keepdims=True) + EPS)


def split_dot(rows, table, dims=None):
    high = rows.astype(BF16)
    low = (rows - high.astype(F32)).astype(BF16)
    both = dot(jnp.concatenate([high.astype(F32), low.astype(F32)], axis=0).astype(BF16), table, dims)
    return both[: rows.shape[0]] + both[rows.shape[0] :]


def iota(shape, axis):
    return lax.broadcasted_iota(jnp.int32, shape, axis)


def kernel(
    patches_hbm, norm_gain_ref, router_ref, in_hbm, out_hbm, post_gain_ref, query_ref, value_hbm, proj_hbm,
    text_ref, heat_ref, intercept_ref,
    pooled_ref, pooled_grad_ref, text_grad_ref,
    patches, w_in, w_out, w_value, w_proj,
    sent, rows, answers, returned, expert_x, hidden, expert_y, normed_buf, dispatch_buf, combine_buf, headed,
    texts, text_pair, units, unit_pair, parts_out, parts_in,
    patch_sem, weight_sem, send_sem, recv_sem, near_send, near_recv,
):
    expert_size = lax.axis_size("expert")
    count = lax.axis_size("dp") * expert_size
    chips = count // 2
    me = lax.axis_index("dp") * expert_size + lax.axis_index("expert")
    core = lax.rem(me, 2)
    chip = me // 2
    sibling = me + 1 - 2 * core
    images, patch_count, width = patches.shape
    slots = router_ref.shape[1]
    heads = query_ref.shape[0]
    groups = images // GROUP

    def place(target):
        return (target // expert_size, lax.rem(target, expert_size))

    patch_copies = [
        pltpu.make_async_copy(patches_hbm.at[i], patches.at[i], patch_sem.at[i]) for i in range(images)
    ]
    weight_copies = [
        pltpu.make_async_copy(source, target, weight_sem.at[n])
        for n, (source, target) in enumerate(
            [(in_hbm.at[0], w_in), (out_hbm.at[0], w_out), (value_hbm, w_value), (proj_hbm, w_proj)]
        )
    ]
    for copy in patch_copies + weight_copies:
        copy.start()

    barrier = pltpu.get_barrier_semaphore()

    @pl.loop(1, count)
    def _(k):
        pl.semaphore_signal(barrier, inc=1, device_id=place(lax.rem(me + k, count)), device_id_type=MESH)

    def to_all(source, target, n):
        @pl.loop(1, count)
        def _(k):
            to = lax.rem(me + k * STRIDE, count)
            pltpu.make_async_remote_copy(
                src_ref=source.at[to], dst_ref=target.at[me], send_sem=send_sem.at[n], recv_sem=recv_sem.at[n],
                device_id=place(to), device_id_type=MESH,
            ).start()

        pltpu.make_async_copy(source.at[me], target.at[me], recv_sem.at[n]).start()

    def from_all(target, n):
        pltpu.make_async_copy(target, target, recv_sem.at[n]).wait()

    def to_class(table, n):
        @pl.loop(1, chips)
        def _(k):
            to = lax.rem(chip + k * STRIDE, chips) * 2 + core
            pltpu.make_async_remote_copy(
                src_ref=table.at[chip], dst_ref=table.at[chip], send_sem=send_sem.at[n], recv_sem=recv_sem.at[n],
                device_id=place(to), device_id_type=MESH,
            ).start()

    def from_class(table, n):
        part = table.at[pl.ds(0, chips - 1)]
        pltpu.make_async_copy(part, part, recv_sem.at[n]).wait()

    def near_copy(source, target, n):
        return pltpu.make_async_remote_copy(
            src_ref=source, dst_ref=target, send_sem=near_send.at[n], recv_sem=near_recv.at[n],
            device_id=place(sibling), device_id_type=MESH,
        )

    norm_gain = norm_gain_ref[...].astype(F32)
    post_gain = post_gain_ref[...].astype(F32)

    def dispatch(group):
        for i in range(GROUP):
            image = group * GROUP + i
            patch_copies[image].wait()
            block = pl.ds(i * patch_count, patch_count)
            normed = layer_norm(patches[image].astype(F32), norm_gain).astype(BF16)
            normed_buf[block, :] = normed
            logits = dot(normed, router_ref[...])
            spread = (iota((slots, GROUP * slots), 1) == GROUP * iota((slots, GROUP * slots), 0) + i)
            spread = spread.astype(F32).astype(BF16)
            weighted = jnp.exp(logits - jnp.max(logits, axis=0, keepdims=True))
            weighted = (weighted / jnp.sum(weighted, axis=0, keepdims=True)).astype(BF16)
            dispatch_buf[block, :] = dot(weighted, spread).astype(BF16)
            mixing = jnp.exp(logits - jnp.max(logits, axis=1, keepdims=True))
            mixing = (mixing / jnp.sum(mixing, axis=1, keepdims=True)).astype(BF16)
            combine_buf[group, block, :] = dot(mixing, spread).astype(BF16)
        slot_in = dot(dispatch_buf[...], normed_buf[...], BY_COLUMNS).astype(BF16)
        sent[group] = slot_in.reshape(slots, GROUP, width)

    def experts(group):
        expert_x[...] = rows[group].reshape(count * GROUP, width)
        inner = w_in.shape[0]
        steps = inner // HIDDEN_STEP

        def hidden_step(first, size):
            pre = dot(expert_x[...], w_in[pl.ds(first, size), :], BY_ROWS)
            hidden[:, pl.ds(first, size)] = jax.nn.gelu(pre, approximate=True).astype(BF16)

        @pl.loop(0, steps)
        def _(k):
            hidden_step(pl.multiple_of(k * HIDDEN_STEP, HIDDEN_STEP), HIDDEN_STEP)

        hidden_step(steps * HIDDEN_STEP, inner - steps * HIDDEN_STEP)

        @pl.loop(0, width // OUT_STEP)
        def _(n):
            columns = pl.ds(pl.multiple_of(n * OUT_STEP, OUT_STEP), OUT_STEP)
            expert_y[:, columns] = dot(hidden[:, 0:inner], w_out[:, columns]).astype(BF16)

        answers[group] = expert_y[...].reshape(count, GROUP, width)

    def pool(group):
        slot_out = returned[group].reshape(slots * GROUP, width)
        for i in range(GROUP):
            image = group * GROUP + i
            block = pl.ds(i * patch_count, patch_count)
            mixed = patches[image].astype(F32) + dot(combine_buf[group, block, :], slot_out)
            pool_in = layer_norm(mixed, post_gain).astype(BF16)
            scores = dot(query_ref[...], pool_in, BY_ROWS)
            attend = jnp.exp(scores - jnp.max(scores, axis=1, keepdims=True))
            mass = jnp.sum(attend, axis=1, keepdims=True)
            headed[pl.ds(image * heads, heads), :] = (dot(attend.astype(BF16), pool_in) / mass).astype(BF16)

    dispatch(0)
    pl.semaphore_wait(barrier, count - 1)
    to_all(sent.at[0], rows.at[0], 0)
    dispatch(1)
    to_all(sent.at[1], rows.at[1], 1)
    weight_copies[0].wait()
    weight_copies[1].wait()
    from_all(rows.at[0], 0)
    experts(0)
    to_all(answers.at[0], returned.at[0], 2)
    from_all(rows.at[1], 1)
    experts(1)
    to_all(answers.at[1], returned.at[1], 3)

    text = text_ref[...]
    texts[chip] = text
    text_pair[0] = text
    to_class(texts, 4)
    near_text = near_copy(text_pair.at[0], text_pair.at[1], 0)
    near_text.start()

    from_all(returned.at[0], 2)
    pool(0)
    weight_copies[2].wait()
    weight_copies[3].wait()
    from_all(returned.at[1], 3)
    pool(1)

    full = dot(headed[...], w_value[...])
    head_width = width // heads
    head = lax.rem(iota(full.shape, 0), heads)
    column = iota(full.shape, 1)
    own_head = (column >= head * head_width) & (column < (head + 1) * head_width)
    values = jnp.sum(jnp.where(own_head, full, 0.0).reshape(images, heads, width), axis=1)
    pooled = dot(values.astype(BF16), w_proj[...])
    pooled_ref[...] = pooled
    img_norm = norm_of(pooled)
    unit = pooled / img_norm
    unit_pair[0] = unit
    near_unit = near_copy(unit_pair.at[0], unit_pair.at[1], 1)
    near_unit.start()
    units[chip] = unit.astype(BF16)
    to_class(units, 5)

    heat = jnp.exp(heat_ref[...])
    intercept = intercept_ref[...]
    pairs = images * count
    side = images * chips
    row, col = iota((2 * images, side), 0), iota((2 * images, side), 1)
    label = jnp.where((row < images) & (col == chip * images + row), 1.0, -1.0)

    def coefficients(cosines):
        scores = heat * cosines + intercept
        return -label * jax.nn.sigmoid(-label * scores) / pairs

    near_text.wait_recv()
    from_class(texts, 4)
    table = texts[...].reshape(side, width)
    table_norm = norm_of(table.astype(F32))
    table_norm = jnp.transpose(jnp.broadcast_to(table_norm, (side, 128)))[0:1, :]
    near_unit.wait_recv()
    cosines = split_dot(unit_pair[...].reshape(2 * images, width), table, BY_ROWS) / table_norm
    part = heat * split_dot(coefficients(cosines) / table_norm, table)
    parts_out[0] = part[images:]
    near_image = near_copy(parts_out.at[0], parts_in.at[0], 2)
    near_image.start()
    image_part = part[:images]

    chip_texts = text_pair[...].reshape(2 * images, width).astype(F32)
    chip_norms = norm_of(chip_texts)
    own_norm = chip_norms[:images]
    own_unit = chip_texts[:images] / own_norm
    near_image.wait_recv()
    grad = image_part + parts_in[0]
    pooled_grad_ref[...] = (grad - unit * jnp.sum(unit * grad, axis=1, keepdims=True)) / img_norm

    from_class(units, 5)
    table = units[...].reshape(side, width)
    cosines = dot(chip_texts.astype(BF16), table, BY_ROWS) / chip_norms
    part = heat * split_dot(coefficients(cosines), table)
    parts_out[1] = part[images:]
    near_words = near_copy(parts_out.at[1], parts_in.at[1], 3)
    near_words.start()
    near_words.wait_recv()
    grad = part[:images] + parts_in[1]
    text_grad_ref[...] = (grad - own_unit * jnp.sum(own_unit * grad, axis=1, keepdims=True)) / own_norm

    for n, buffer in enumerate([sent.at[0], sent.at[1], answers.at[0], answers.at[1]]):
        part_ref = buffer.at[pl.ds(0, count - 1)]
        pltpu.make_async_copy(part_ref, part_ref, send_sem.at[n]).wait()
    for n, buffer in [(4, texts), (5, units)]:
        part_ref = buffer.at[pl.ds(0, chips - 1)]
        pltpu.make_async_copy(part_ref, part_ref, send_sem.at[n]).wait()
    for copy in (near_text, near_unit, near_image, near_words):
        copy.wait_send()


def body(
    patches, norm_gain, router, expert_in, expert_out, post_gain, key_query, value_proj, out_proj, text_embed,
    inverse_heat_exponent, score_intercept,
):
    images, patch_count, width = patches.shape
    inner = expert_out.shape[1]
    slots, heads = router.shape[1], key_query.shape[0]
    count = lax.axis_size("dp") * lax.axis_size("expert")
    chips = count // 2
    groups = images // GROUP
    vmem = pl.BlockSpec(memory_space=pltpu.VMEM)
    hbm = pl.BlockSpec(memory_space=pl.ANY)
    inner_padded = -(-inner // 128) * 128
    traffic = (groups, count, GROUP, width)
    out = jax.ShapeDtypeStruct((images, width), F32)
    return pl.pallas_call(
        kernel,
        out_shape=(out, out, out),
        in_specs=[hbm, vmem, vmem, hbm, hbm, vmem, vmem, hbm, hbm, vmem, vmem, vmem],
        out_specs=(vmem, vmem, vmem),
        scratch_shapes=[
            pltpu.VMEM(patches.shape, BF16),
            pltpu.VMEM((inner, width), BF16),
            pltpu.VMEM((inner, width), BF16),
            pltpu.VMEM(value_proj.shape, BF16),
            pltpu.VMEM(out_proj.shape, BF16),
            pltpu.VMEM(traffic, BF16),
            pltpu.VMEM(traffic, BF16),
            pltpu.VMEM(traffic, BF16),
            pltpu.VMEM(traffic, BF16),
            pltpu.VMEM((count * GROUP, width), BF16),
            pltpu.VMEM((count * GROUP, inner_padded), BF16),
            pltpu.VMEM((count * GROUP, width), BF16),
            pltpu.VMEM((GROUP * patch_count, width), BF16),
            pltpu.VMEM((GROUP * patch_count, GROUP * slots), BF16),
            pltpu.VMEM((groups, GROUP * patch_count, GROUP * slots), BF16),
            pltpu.VMEM((images * heads, width), BF16),
            pltpu.VMEM((chips, images, width), BF16),
            pltpu.VMEM((2, images, width), BF16),
            pltpu.VMEM((chips, images, width), BF16),
            pltpu.VMEM((2, images, width), F32),
            pltpu.VMEM((2, images, width), F32),
            pltpu.VMEM((2, images, width), F32),
            pltpu.SemaphoreType.DMA((images,)),
            pltpu.SemaphoreType.DMA((4,)),
            pltpu.SemaphoreType.DMA((6,)),
            pltpu.SemaphoreType.DMA((6,)),
            pltpu.SemaphoreType.DMA((4,)),
            pltpu.SemaphoreType.DMA((4,)),
        ],
        compiler_params=pltpu.CompilerParams(
            collective_id=0, has_side_effects=True, vmem_limit_bytes=60 * 1024 * 1024
        ),
        cost_estimate=pl.CostEstimate(flops=12_000_000_000, bytes_accessed=40_000_000, transcendentals=4_000_000),
    )(
        patches, norm_gain.reshape(1, width), router, jnp.swapaxes(expert_in, 1, 2), expert_out,
        post_gain.reshape(1, width), key_query, value_proj, out_proj, text_embed,
        inverse_heat_exponent.reshape(1, 1), score_intercept.reshape(1, 1),
    )


def solution(mesh):
    split = ("dp", "expert")
    placed = (
        P(split, None, None), P(), P(), P(split, None, None), P(split, None, None), P(), P(), P(), P(),
        P(split, None), P(), P(),
    )
    return jax.shard_map(
        body, mesh=mesh, in_specs=placed,
        out_specs=(P(split, None), P(split, None), P(split, None)), check_vma=False,
    )
```

time: 343 us -> 83.2 us (0.24); the launches traced: 338 us -> 82.9 us
  waiting for transfers between devices: 168 us -> 0 us
  Pallas kernels: 0 us -> 74.4 us
  matrix products: 61.2 us -> 0 us
  blocking collectives: 32 us -> 0 us
  other arithmetic: 24.6 us -> 0 us
  local copies, waits for them, and re-layouts: 30.6 us -> 6.55 us
  between operations: 15.8 us -> 1.93 us
  starting transfers between devices: 5.7 us -> 0 us
    unnamed x3 -> x0, waiting for transfers between devices: 145 us -> none
    pallas_call x0 -> x1, Pallas kernels: none -> 74.4 us  [body(): pl.pallas_call(kernel, out_shape=(out, out, out), in_specs=[hbm, vmem, vm...]
    dot_general x11 -> x0, matrix products: 61.2 us -> none  [the longest x1 31.8 us: run_experts(): jnp.einsum('nkf,kfd->nkd', hidden, expert_out, preferred_element_type=jnp...]
    all_to_all x1 -> x0, blocking collectives: 32 us -> none  [body(): lax.all_to_all(slot_in, ('dp', 'expert'), split_axis=1, concat_axis=0, ti...]
    unnamed x21 -> x3, local copies, waits for them, and re-layouts: 17.9 us -> 3.99 us
    all_to_all x1 -> x0, waiting for transfers between devices: 12.6 us -> none  [body(): lax.all_to_all(answers, ('dp', 'expert'), split_axis=0, concat_axis=1, ti...]
    all_gather x1 -> x0, waiting for transfers between devices: 10.6 us -> none  [body(): lax.all_gather(text_embed, ('dp', 'expert'), axis=0, tiled=True)]
    all_to_all x1 -> x0, other arithmetic: 9.21 us -> none  [body(): lax.all_to_all(answers, ('dp', 'expert'), split_axis=0, concat_axis=1, ti...]
  transfers between devices with their start and end apart: 3 -> 0, of which waited for: 3 -> 0; matrix products, arithmetic and copies ran while one was open for 13% -> 0% of each run, Pallas kernels for 0% -> 0%
where the time goes in v1:
time: 83.2 us; the launch traced here: 82.9 us
  Pallas kernels  74.4 us (89%)
  local copies, waits for them, and re-layouts  6.55 us (8%)
  between operations  1.93 us (2%)
    pallas_call x1, Pallas kernels, body(): pl.pallas_call(kernel, out_shape=(out, out, out), in_specs=[hbm, vmem, vm...  74.4 us
    unnamed x3, local copies, waits for them, and re-layouts  3.99 us

profile of v1, /device:TPU:1, one launch (start us, length us, event | category | flops | bytes accessed | tf_op | source)
XLA Modules:
  0.0 82.9 jit_solution(5362118412029789025)
XLA Ops:
  1.9 1.3 %reshape.18.norm_gain_ref = bf16[1,1152]{1,0:T(2,128)(2,1)} reshape(bf16[1152]{0:T(1024)(128)(2,1)} %param.13) | data formatting | bytes 4608 | tf_op jit(solution)/shard_map/reshape | solution.py:332
  3.2 1.3 %reshape.19.post_gain_ref = bf16[1,1152]{1,0:T(2,128)(2,1)} reshape(bf16[1152]{0:T(1024)(128)(2,1)} %param.17) | data formatting | bytes 4608 | tf_op jit(solution)/shard_map/reshape | solution.py:333
  4.5 74.4 %shard_map.139 = (f32[4,1152]{1,0:T(4,128)}, f32[4,1152]{1,0:T(4,128)}, f32[4,1152]{1,0:T(4,128)}) custom-call(bf16[4,256,1152]{2,1,0:T(8,128)(2,1)} %patches_hbm.1, bf16[1,1152]{1,0:T(2,128)(2,1)} %reshape.18.norm_gain_ref, bf16[1152,128]{1,0:T(8,128)(2,1)} %router_ref.1, bf16[1,4304,1152]{2,1,0:T(8,128)(2,1)} %bitcast.5, bf16[1,4304,1152]{2,1,0:T(8,128)(2,1)} %out_hbm.1, ...), custom_call_target="tpu_custom_call" | custom-call | flops 12000000000 | bytes 40000000 | tf_op jit(solution)/shard_map/pallas_call | solution.py:292
  78.9 1.3 %copy.20 = f32[4,1152]{1,0:T(4,128)} copy(f32[4,1152]{1,0:T(4,128)} %get-tuple-element.6) | data formatting | bytes 36864
  80.2 1.3 %copy.21 = f32[4,1152]{1,0:T(4,128)} copy(f32[4,1152]{1,0:T(4,128)} %get-tuple-element.7) | data formatting | bytes 36864
  81.5 1.3 %copy.22 = f32[4,1152]{1,0:T(4,128)} copy(f32[4,1152]{1,0:T(4,128)} %get-tuple-element.8) | data formatting | bytes 36864

commit v2 on v1

v2 whole, which is shorter than its diff:
```python
import functools

import jax
import jax.numpy as jnp
from jax import lax
from jax.experimental import pallas as pl
from jax.experimental.pallas import tpu as pltpu
from jax.sharding import PartitionSpec as P

MESH = pl.DeviceIdType.MESH
BF16, F32 = jnp.bfloat16, jnp.float32
BY_ROWS = (((1,), (1,)), ((), ()))
BY_COLUMNS = (((0,), (0,)), ((), ()))
EPS = 1e-6
GROUP = 2
STRIDE = 37
RING = 8
HIDDEN_STEP = 2176
VMEM_BYTES = 60 * 1024 * 1024


def dot(a, b, dims=None):
    if dims is None:
        return jnp.dot(a, b, preferred_element_type=F32)
    return lax.dot_general(a, b, dims, preferred_element_type=F32)


def layer_norm(inputs, gain):
    center = jnp.mean(inputs, axis=1, keepdims=True)
    shifted = inputs - center
    spread = jnp.mean(shifted * shifted, axis=1, keepdims=True)
    return shifted * lax.rsqrt(spread + EPS) * gain


def norm_of(rows):
    return jnp.sqrt(jnp.sum(rows * rows, axis=1, keepdims=True) + EPS)


def split_dot(rows, table, dims=None):
    high = rows.astype(BF16)
    low = (rows - high.astype(F32)).astype(BF16)
    both = dot(jnp.concatenate([high.astype(F32), low.astype(F32)], axis=0).astype(BF16), table, dims)
    return both[: rows.shape[0]] + both[rows.shape[0] :]


def iota(shape, axis):
    return lax.broadcasted_iota(jnp.int32, shape, axis)


def kernel(
    patches_hbm, norm_gain_hbm, router_hbm, in_hbm, out_hbm, post_gain_hbm, query_hbm, value_hbm, proj_hbm,
    text_hbm, heat_ref, intercept_ref,
    result_ref,
    norm_gain_ref, router_ref, post_gain_ref, query_ref, text_ref,
    patches, w_in, w_out, w_value, w_proj,
    sent, rows, answers, returned, expert_x, hidden, normed_buf, dispatch_buf, combine_buf, headed,
    line_texts, texts, line_units, units, image_parts, image_sums, text_parts, text_sums,
    patch_sem, weight_sem, small_sem, send_sem, recv_sem,
):
    expert_size = lax.axis_size("expert")
    count = lax.axis_size("dp") * expert_size
    lines = count // RING
    me = lax.axis_index("dp") * expert_size + lax.axis_index("expert")
    line, spot = me // RING, lax.rem(me, RING)
    images, patch_count, width = patches.shape
    slots = router_ref.shape[1]
    heads = query_ref.shape[0]
    groups = images // GROUP

    def place(target):
        return (target // expert_size, lax.rem(target, expert_size))

    patch_copies = [
        pltpu.make_async_copy(patches_hbm.at[i], patches.at[i], patch_sem.at[i]) for i in range(images)
    ]
    inner_rows = pl.ds(0, in_hbm.shape[1])
    weight_copies = [
        pltpu.make_async_copy(source, target, weight_sem.at[n])
        for n, (source, target) in enumerate(
            [(in_hbm.at[0], w_in.at[inner_rows]), (out_hbm.at[0], w_out.at[inner_rows]), (value_hbm, w_value), (proj_hbm, w_proj)]
        )
    ]
    small_copies = [
        pltpu.make_async_copy(source, target, small_sem.at[n])
        for n, (source, target) in enumerate(
            [
                (norm_gain_hbm, norm_gain_ref), (router_hbm, router_ref), (post_gain_hbm, post_gain_ref),
                (query_hbm, query_ref), (text_hbm, text_ref),
            ]
        )
    ]
    for copy in patch_copies[:1] + small_copies + patch_copies[1:]:
        copy.start()
    for copy in weight_copies:
        copy.start(priority=1)

    barrier = pltpu.get_barrier_semaphore()

    @pl.loop(1, count)
    def _(k):
        pl.semaphore_signal(barrier, inc=1, device_id=place(lax.rem(me + k, count)), device_id_type=MESH)

    def to_all(source, target, n):
        @pl.loop(1, count)
        def _(k):
            to = lax.rem(me + k * STRIDE, count)
            pltpu.make_async_remote_copy(
                src_ref=source.at[to], dst_ref=target.at[me], send_sem=send_sem.at[n], recv_sem=recv_sem.at[n],
                device_id=place(to), device_id_type=MESH,
            ).start()

        pltpu.make_async_copy(source.at[me], target.at[me], recv_sem.at[n]).start()

    def have_left(buffer, n):
        part = buffer.at[pl.ds(0, buffer.shape[0] - 1)]
        pltpu.make_async_copy(part, part, send_sem.at[n]).wait()

    def from_all(target, n):
        pltpu.make_async_copy(target, target, recv_sem.at[n]).wait()

    def to_line(source, target, n):
        @pl.loop(1, RING)
        def _(k):
            to = lax.rem(spot + k, RING)
            pltpu.make_async_remote_copy(
                src_ref=source.at[to] if len(source.shape) == 3 else source, dst_ref=target.at[spot],
                send_sem=send_sem.at[n], recv_sem=recv_sem.at[n],
                device_id=place(line * RING + to), device_id_type=MESH,
            ).start()

    def to_lines(table, n):
        @pl.loop(1, lines)
        def _(k):
            to = lax.rem(line + k * 5, lines)
            pltpu.make_async_remote_copy(
                src_ref=table.at[line], dst_ref=table.at[line], send_sem=send_sem.at[n], recv_sem=recv_sem.at[n],
                device_id=place(to * RING + spot), device_id_type=MESH,
            ).start()

    def from_others(table, n):
        part = table.at[pl.ds(0, table.shape[0] - 1)]
        pltpu.make_async_copy(part, part, recv_sem.at[n]).wait()

    for copy in small_copies:
        copy.wait()
    norm_gain = norm_gain_ref[...].astype(F32).reshape(1, width)
    post_gain = post_gain_ref[...].astype(F32).reshape(1, width)

    def patch_wait(image):
        pltpu.make_async_copy(patches_hbm.at[image], patches.at[image], patch_sem.at[image]).wait()

    def spreading(i):
        shape = (slots, GROUP * slots)
        return (iota(shape, 1) == GROUP * iota(shape, 0) + i).astype(F32).astype(BF16)

    def block_of(i):
        return pl.ds(pl.multiple_of(i * patch_count, patch_count), patch_count)

    def dispatch(group):
        @pl.loop(0, GROUP)
        def _(i):
            image = group * GROUP + i
            block = block_of(i)
            patch_wait(image)
            normed = layer_norm(patches[image].astype(F32), norm_gain).astype(BF16)
            normed_buf[block, :] = normed
            logits = dot(normed, router_ref[...])
            spread = spreading(i)
            weighted = jnp.exp(logits - jnp.max(logits, axis=0, keepdims=True))
            weighted = (weighted / jnp.sum(weighted, axis=0, keepdims=True)).astype(BF16)
            dispatch_buf[block, :] = dot(weighted, spread).astype(BF16)
            mixing = jnp.exp(logits - jnp.max(logits, axis=1, keepdims=True))
            mixing = (mixing / jnp.sum(mixing, axis=1, keepdims=True)).astype(BF16)
            combine_buf[group, block, :] = dot(mixing, spread).astype(BF16)

        slot_in = dot(dispatch_buf[...], normed_buf[...], BY_COLUMNS).astype(BF16)
        sent[group] = slot_in.reshape(slots, GROUP, width)

    def experts(group):
        expert_x[...] = rows[group].reshape(count * GROUP, width)

        @pl.loop(0, hidden.shape[1] // HIDDEN_STEP)
        def _(k):
            part = pl.ds(pl.multiple_of(k * HIDDEN_STEP, HIDDEN_STEP), HIDDEN_STEP)
            pre = dot(expert_x[...], w_in[part, :], BY_ROWS)
            hidden[:, part] = jax.nn.gelu(pre, approximate=True).astype(BF16)

        answers[group] = dot(hidden[...], w_out[...]).astype(BF16).reshape(count, GROUP, width)

    def pool(group):
        @pl.loop(0, GROUP)
        def _(i):
            image = group * GROUP + i
            slot_out = returned[group].reshape(slots * GROUP, width)
            mixed = patches[image].astype(F32) + dot(combine_buf[group, block_of(i), :], slot_out)
            pool_in = layer_norm(mixed, post_gain).astype(BF16)
            scores = dot(query_ref[...], pool_in, BY_ROWS)
            attend = jnp.exp(scores - jnp.max(scores, axis=1, keepdims=True))
            mass = jnp.sum(attend, axis=1, keepdims=True)
            summed = dot(attend.astype(BF16), pool_in) / mass
            headed[pl.ds(pl.multiple_of(image * heads, heads), heads), :] = summed.astype(BF16)

    inner = in_hbm.shape[1]
    filler = w_in.shape[0] - inner
    w_in[pl.ds(inner, filler), :] = jnp.zeros((filler, width), BF16)
    w_out[pl.ds(inner, filler), :] = jnp.zeros((filler, width), BF16)

    @pl.loop(0, groups)
    def _(group):
        dispatch(group)

        @pl.when(group == 0)
        def _():
            pl.semaphore_wait(barrier, count - 1)

        @pl.when(group > 0)
        def _():
            have_left(sent.at[0], 0)

        to_all(sent.at[group], rows.at[group], group)

    weight_copies[0].wait()
    weight_copies[1].wait()

    @pl.loop(0, groups)
    def _(group):
        from_all(rows.at[group], group)
        experts(group)
        to_all(answers.at[group], returned.at[group], groups + group)

    text = text_ref[...]
    line_texts[spot] = text
    texts[line] = text
    to_line(line_texts.at[spot], line_texts, 4)
    to_lines(texts, 5)
    weight_copies[2].wait()
    weight_copies[3].wait()

    @pl.loop(0, groups)
    def _(group):
        from_all(returned.at[group], groups + group)
        pool(group)

    full = dot(headed[...], w_value[...])
    head_width = width // heads
    head = lax.rem(iota(full.shape, 0), heads)
    column = iota(full.shape, 1)
    own_head = (column >= head * head_width) & (column < (head + 1) * head_width)
    values = jnp.sum(jnp.where(own_head, full, 0.0).reshape(images, heads, width), axis=1)
    pooled = dot(values.astype(BF16), w_proj[...])
    result_ref[0] = pooled
    img_norm = norm_of(pooled)
    unit = pooled / img_norm
    line_units[spot] = unit.astype(BF16)
    units[line] = unit.astype(BF16)
    to_line(line_units.at[spot], line_units, 6)
    to_lines(units, 7)

    heat = jnp.exp(jnp.full((1, 1), heat_ref[0], F32))
    intercept = intercept_ref[0]
    pairs = images * count
    near, far = images * RING, images * lines
    row, col = iota((near, far), 0), iota((near, far), 1)
    own_row = (row >= spot * images) & (row < (spot + 1) * images)
    label = jnp.where(own_row & (row - spot * images == col - line * images), 1.0, -1.0)

    zeros = jnp.zeros((images, width), BF16)
    image_sums[spot] = zeros
    text_sums[spot] = zeros

    def own_block(part):
        return jnp.sum(jnp.where(own_row[:, 0:1], part, 0.0).reshape(RING, images, width), axis=0)

    def coefficients(cosines):
        scores = heat * cosines + intercept
        return -label * jax.nn.sigmoid(-label * scores) / pairs

    from_others(line_texts, 4)
    from_others(texts, 5)
    table = texts[...].reshape(far, width)
    table_norm = norm_of(table.astype(F32))
    table_norm = jnp.transpose(jnp.broadcast_to(table_norm, (far, 128)))[0:1, :]
    near_texts = line_texts[...].reshape(near, width)
    near_norms = norm_of(near_texts.astype(F32))
    text = text.astype(F32)
    text_norm = norm_of(text)
    unit_text = text / text_norm
    from_others(line_units, 6)
    cosines = dot(line_units[...].reshape(near, width), table, BY_ROWS) / table_norm
    part = heat * split_dot(coefficients(cosines) / table_norm, table)
    image_parts[...] = part.astype(BF16).reshape(RING, images, width)
    to_line(image_parts, image_sums, 8)
    own_image_part = own_block(part)

    from_others(units, 7)
    table = units[...].reshape(far, width)
    cosines = dot(near_texts, table, BY_ROWS) / near_norms
    part = heat * split_dot(coefficients(cosines), table)
    text_parts[...] = part.astype(BF16).reshape(RING, images, width)
    to_line(text_parts, text_sums, 9)
    own_text_part = own_block(part)

    from_others(image_sums, 8)
    grad = own_image_part + jnp.sum(image_sums[...].astype(F32), axis=0)
    result_ref[1] = (grad - unit * jnp.sum(unit * grad, axis=1, keepdims=True)) / img_norm
    from_others(text_sums, 9)
    grad = own_text_part + jnp.sum(text_sums[...].astype(F32), axis=0)
    result_ref[2] = (grad - unit_text * jnp.sum(unit_text * grad, axis=1, keepdims=True)) / text_norm

    blocks = [
        sent.at[1], answers.at[0], answers.at[1], line_texts, texts, line_units, units, image_parts, text_parts,
    ]
    for n, buffer in enumerate(blocks):
        have_left(buffer, n + 1)


def unstack(stacked_ref, pooled_ref, pooled_grad_ref, text_grad_ref, sem):
    copies = [
        pltpu.make_async_copy(stacked_ref.at[n], target, sem.at[n])
        for n, target in enumerate((pooled_ref, pooled_grad_ref, text_grad_ref))
    ]
    for copy in copies:
        copy.start()
    for copy in copies:
        copy.wait()


def body(
    patches, norm_gain, router, expert_in, expert_out, post_gain, key_query, value_proj, out_proj, text_embed,
    inverse_heat_exponent, score_intercept,
):
    images, patch_count, width = patches.shape
    inner = expert_out.shape[1]
    slots, heads = router.shape[1], key_query.shape[0]
    count = lax.axis_size("dp") * lax.axis_size("expert")
    groups = images // GROUP
    vmem = pl.BlockSpec(memory_space=pltpu.VMEM)
    hbm = pl.BlockSpec(memory_space=pl.ANY)
    filled = -(-inner // HIDDEN_STEP) * HIDDEN_STEP
    traffic = (groups, count, GROUP, width)
    out = jax.ShapeDtypeStruct((images, width), F32)
    result = pl.pallas_call(
        kernel,
        out_shape=jax.ShapeDtypeStruct((3, images, width), F32),
        in_specs=[hbm] * 10 + [pl.BlockSpec(memory_space=pltpu.SMEM)] * 2,
        out_specs=vmem,
        scratch_shapes=[
            pltpu.VMEM((width,), BF16),
            pltpu.VMEM(router.shape, BF16),
            pltpu.VMEM((width,), BF16),
            pltpu.VMEM(key_query.shape, BF16),
            pltpu.VMEM(text_embed.shape, BF16),
            pltpu.VMEM(patches.shape, BF16),
            pltpu.VMEM((filled, width), BF16),
            pltpu.VMEM((filled, width), BF16),
            pltpu.VMEM(value_proj.shape, BF16),
            pltpu.VMEM(out_proj.shape, BF16),
            pltpu.VMEM(traffic, BF16),
            pltpu.VMEM(traffic, BF16),
            pltpu.VMEM(traffic, BF16),
            pltpu.VMEM(traffic, BF16),
            pltpu.VMEM((count * GROUP, width), BF16),
            pltpu.VMEM((count * GROUP, filled), BF16),
            pltpu.VMEM((GROUP * patch_count, width), BF16),
            pltpu.VMEM((GROUP * patch_count, GROUP * slots), BF16),
            pltpu.VMEM((groups, GROUP * patch_count, GROUP * slots), BF16),
            pltpu.VMEM((images * heads, width), BF16),
            pltpu.VMEM((RING, images, width), BF16),
            pltpu.VMEM((count // RING, images, width), BF16),
            pltpu.VMEM((RING, images, width), BF16),
            pltpu.VMEM((count // RING, images, width), BF16),
            pltpu.VMEM((RING, images, width), BF16),
            pltpu.VMEM((RING, images, width), BF16),
            pltpu.VMEM((RING, images, width), BF16),
            pltpu.VMEM((RING, images, width), BF16),
            pltpu.SemaphoreType.DMA((images,)),
            pltpu.SemaphoreType.DMA((4,)),
            pltpu.SemaphoreType.DMA((5,)),
            pltpu.SemaphoreType.DMA((10,)),
            pltpu.SemaphoreType.DMA((10,)),
        ],
        compiler_params=pltpu.CompilerParams(
            collective_id=0, has_side_effects=True, vmem_limit_bytes=VMEM_BYTES
        ),
        cost_estimate=pl.CostEstimate(flops=12_000_000_000, bytes_accessed=40_000_000, transcendentals=4_000_000),
    )(
        patches, norm_gain, router, jnp.swapaxes(expert_in, 1, 2), expert_out, post_gain, key_query, value_proj,
        out_proj, text_embed, inverse_heat_exponent, score_intercept,
    )
    return pl.pallas_call(
        unstack,
        out_shape=(out, out, out),
        in_specs=[hbm],
        out_specs=(hbm, hbm, hbm),
        scratch_shapes=[pltpu.SemaphoreType.DMA((3,))],
        compiler_params=pltpu.CompilerParams(vmem_limit_bytes=VMEM_BYTES),
    )(result)


def solution(mesh):
    split = ("dp", "expert")
    placed = (
        P(split, None, None), P(), P(), P(split, None, None), P(split, None, None), P(), P(), P(), P(),
        P(split, None), P(), P(),
    )
    return jax.shard_map(
        body, mesh=mesh, in_specs=placed,
        out_specs=(P(split, None), P(split, None), P(split, None)), check_vma=False,
    )
```

time: 83.2 us -> 69.1 us (0.83)
  Pallas kernels: 74.4 us -> 67 us
  local copies, waits for them, and re-layouts: 6.55 us -> 0 us
    pallas_call x1 -> x2, Pallas kernels: 74.4 us -> 67 us  [the longest x1 64.2 us: body(): pl.pallas_call(kernel, out_shape=jax.ShapeDtypeStruct((3, images, width),...]
    unnamed x3 -> x0, local copies, waits for them, and re-layouts: 3.99 us -> none
    reshape x2 -> x0, local copies, waits for them, and re-layouts: 2.57 us -> none  [the longest x1 1.28 us: body(): norm_gain.reshape(1, width)]
where the time goes in v2:
time: 69.1 us; the launch traced here: 68.9 us
  Pallas kernels  67 us (97%)
  between operations  1.93 us (3%)
    pallas_call x1, Pallas kernels, body(): pl.pallas_call(kernel, out_shape=jax.ShapeDtypeStruct((3, images, width),...  64.2 us
    pallas_call x1, Pallas kernels, body(): pl.pallas_call(unstack, out_shape=(out, out, out), in_specs=[hbm], out_sp...  2.8 us

profile of v2, /device:TPU:1, one launch (start us, length us, event | category | flops | bytes accessed | tf_op | source)
XLA Modules:
  0.0 68.9 jit_solution(12818365896663424531)
XLA Ops:
  1.9 64.2 %shard_map.139.stacked_ref = f32[3,4,1152]{2,1,0:T(4,128)} custom-call(bf16[4,256,1152]{2,1,0:T(8,128)(2,1)} %patches_hbm.1, bf16[1152]{0:T(1024)(128)(2,1)} %norm_gain_hbm.1, bf16[1152,128]{1,0:T(8,128)(2,1)} %router_hbm.1, bf16[1,4304,1152]{2,1,0:T(8,128)(2,1)} %bitcast.1, bf16[1,4304,1152]{2,1,0:T(8,128)(2,1)} %out_hbm.1, bf16[1152]{0:T(1024)(128)(2,1)} %post_gain_hbm.1, ...), custom_call_target="tpu_custom_call" | custom-call | flops 12000000000 | bytes 40000000 | tf_op jit(solution)/shard_map/pallas_call | solution.py:342
  66.1 2.8 %shard_map.140 = (f32[4,1152]{1,0:T(4,128)}, f32[4,1152]{1,0:T(4,128)}, f32[4,1152]{1,0:T(4,128)}) custom-call(f32[3,4,1152]{2,1,0:T(4,128)} %shard_map.139.stacked_ref), custom_call_target="tpu_custom_call" | custom-call | tf_op jit(solution)/shard_map/pallas_call | solution.py:390

commit v3 on v2

--- a/solution.py
+++ b/solution.py
@@ -15,7 +15,7 @@
 GROUP = 2
 STRIDE = 37
 RING = 8
-HIDDEN_STEP = 2176
+HIDDEN_STEP = 4352
 VMEM_BYTES = 60 * 1024 * 1024
 
 
@@ -188,11 +188,10 @@
         answers[group] = dot(hidden[...], w_out[...]).astype(BF16).reshape(count, GROUP, width)
 
     def pool(group):
-        @pl.loop(0, GROUP)
-        def _(i):
+        for i in range(GROUP):
             image = group * GROUP + i
             slot_out = returned[group].reshape(slots * GROUP, width)
-            mixed = patches[image].astype(F32) + dot(combine_buf[group, block_of(i), :], slot_out)
+            mixed = patches[image].astype(F32) + dot(combine_buf[group, pl.ds(i * patch_count, patch_count), :], slot_out)
             pool_in = layer_norm(mixed, post_gain).astype(BF16)
             scores = dot(query_ref[...], pool_in, BY_ROWS)
             attend = jnp.exp(scores - jnp.max(scores, axis=1, keepdims=True))
@@ -228,11 +227,14 @@
         experts(group)
         to_all(answers.at[group], returned.at[group], groups + group)
 
+        @pl.when(group == 0)
+        def _():
+            line_texts[spot] = text_ref[...]
+            texts[line] = text_ref[...]
+            to_line(line_texts.at[spot], line_texts, 4)
+            to_lines(texts, 5)
+
     text = text_ref[...]
-    line_texts[spot] = text
-    texts[line] = text
-    to_line(line_texts.at[spot], line_texts, 4)
-    to_lines(texts, 5)
     weight_copies[2].wait()
     weight_copies[3].wait()
 

time: 69.1 us -> 67.1 us (0.971)
  Pallas kernels: 67 us -> 65.1 us
    pallas_call x1, Pallas kernels: 64.2 us -> 62.3 us  [body(): pl.pallas_call(kernel, out_shape=jax.ShapeDtypeStruct((3, images, width),...]
where the time goes in v3:
time: 67.1 us; the launch traced here: 67 us
  Pallas kernels  65.1 us (97%)
  between operations  1.93 us (3%)
    pallas_call x1, Pallas kernels, body(): pl.pallas_call(kernel, out_shape=jax.ShapeDtypeStruct((3, images, width),...  62.3 us
    pallas_call x1, Pallas kernels, body(): pl.pallas_call(unstack, out_shape=(out, out, out), in_specs=[hbm], out_sp...  2.8 us

profile of v3, /device:TPU:1, one launch (start us, length us, event | category | flops | bytes accessed | tf_op | source)
XLA Modules:
  0.0 67.0 jit_solution(5327176308027535773)
XLA Ops:
  1.9 62.3 %shard_map.139.stacked_ref = f32[3,4,1152]{2,1,0:T(4,128)} custom-call(bf16[4,256,1152]{2,1,0:T(8,128)(2,1)} %patches_hbm.1, bf16[1152]{0:T(1024)(128)(2,1)} %norm_gain_hbm.1, bf16[1152,128]{1,0:T(8,128)(2,1)} %router_hbm.1, bf16[1,4304,1152]{2,1,0:T(8,128)(2,1)} %bitcast.1, bf16[1,4304,1152]{2,1,0:T(8,128)(2,1)} %out_hbm.1, bf16[1152]{0:T(1024)(128)(2,1)} %post_gain_hbm.1, ...), custom_call_target="tpu_custom_call" | custom-call | flops 12000000000 | bytes 40000000 | tf_op jit(solution)/shard_map/pallas_call | solution.py:344
  64.2 2.8 %shard_map.140 = (f32[4,1152]{1,0:T(4,128)}, f32[4,1152]{1,0:T(4,128)}, f32[4,1152]{1,0:T(4,128)}) custom-call(f32[3,4,1152]{2,1,0:T(4,128)} %shard_map.139.stacked_ref), custom_call_target="tpu_custom_call" | custom-call | tf_op jit(solution)/shard_map/pallas_call | solution.py:392

commit v4 on v3

--- a/solution.py
+++ b/solution.py
@@ -14,6 +14,7 @@
 EPS = 1e-6
 GROUP = 2
 STRIDE = 37
+SEND_BATCH = 14
 RING = 8
 HIDDEN_STEP = 4352
 VMEM_BYTES = 60 * 1024 * 1024
@@ -101,13 +102,22 @@
         pl.semaphore_signal(barrier, inc=1, device_id=place(lax.rem(me + k, count)), device_id_type=MESH)
 
     def to_all(source, target, n):
-        @pl.loop(1, count)
-        def _(k):
+        def send(k):
             to = lax.rem(me + k * STRIDE, count)
             pltpu.make_async_remote_copy(
                 src_ref=source.at[to], dst_ref=target.at[me], send_sem=send_sem.at[n], recv_sem=recv_sem.at[n],
                 device_id=place(to), device_id_type=MESH,
             ).start()
+
+        batches = (count - 1) // SEND_BATCH
+
+        @pl.loop(0, batches)
+        def _(batch):
+            for k in range(SEND_BATCH):
+                send(batch * SEND_BATCH + k + 1)
+
+        for k in range(batches * SEND_BATCH + 1, count):
+            send(k)
 
         pltpu.make_async_copy(source.at[me], target.at[me], recv_sem.at[n]).start()
 

time: 67.1 us -> 66.1 us (0.985)
  Pallas kernels: 65.1 us -> 64.1 us
    pallas_call x1, Pallas kernels: 62.3 us -> 61.3 us  [body(): pl.pallas_call(kernel, out_shape=jax.ShapeDtypeStruct((3, images, width),...]
where the time goes in v4:
time: 66.1 us; the launch traced here: 66 us
  Pallas kernels  64.1 us (97%)
  between operations  1.93 us (3%)
    pallas_call x1, Pallas kernels, body(): pl.pallas_call(kernel, out_shape=jax.ShapeDtypeStruct((3, images, width),...  61.3 us
    pallas_call x1, Pallas kernels, body(): pl.pallas_call(unstack, out_shape=(out, out, out), in_specs=[hbm], out_sp...  2.8 us

profile of v4, /device:TPU:1, one launch (start us, length us, event | category | flops | bytes accessed | tf_op | source)
XLA Modules:
  0.0 66.0 jit_solution(5907348686752982472)
XLA Ops:
  1.9 61.3 %shard_map.139.stacked_ref = f32[3,4,1152]{2,1,0:T(4,128)} custom-call(bf16[4,256,1152]{2,1,0:T(8,128)(2,1)} %patches_hbm.1, bf16[1152]{0:T(1024)(128)(2,1)} %norm_gain_hbm.1, bf16[1152,128]{1,0:T(8,128)(2,1)} %router_hbm.1, bf16[1,4304,1152]{2,1,0:T(8,128)(2,1)} %bitcast.1, bf16[1,4304,1152]{2,1,0:T(8,128)(2,1)} %out_hbm.1, bf16[1152]{0:T(1024)(128)(2,1)} %post_gain_hbm.1, ...), custom_call_target="tpu_custom_call" | custom-call | flops 12000000000 | bytes 40000000 | tf_op jit(solution)/shard_map/pallas_call | solution.py:354
  63.2 2.8 %shard_map.140 = (f32[4,1152]{1,0:T(4,128)}, f32[4,1152]{1,0:T(4,128)}, f32[4,1152]{1,0:T(4,128)}) custom-call(f32[3,4,1152]{2,1,0:T(4,128)} %shard_map.139.stacked_ref), custom_call_target="tpu_custom_call" | custom-call | tf_op jit(solution)/shard_map/pallas_call | solution.py:402

commit v5 on v4

--- a/solution.py
+++ b/solution.py
@@ -129,8 +129,7 @@
         pltpu.make_async_copy(target, target, recv_sem.at[n]).wait()
 
     def to_line(source, target, n):
-        @pl.loop(1, RING)
-        def _(k):
+        for k in range(1, RING):
             to = lax.rem(spot + k, RING)
             pltpu.make_async_remote_copy(
                 src_ref=source.at[to] if len(source.shape) == 3 else source, dst_ref=target.at[spot],
@@ -139,8 +138,7 @@
             ).start()
 
     def to_lines(table, n):
-        @pl.loop(1, lines)
-        def _(k):
+        for k in range(1, lines):
             to = lax.rem(line + k * 5, lines)
             pltpu.make_async_remote_copy(
                 src_ref=table.at[line], dst_ref=table.at[line], send_sem=send_sem.at[n], recv_sem=recv_sem.at[n],

time: 66.1 us -> 65.8 us (level)
  no operation moved by 1% of the time
where the time goes in v5:
time: 65.8 us; the launch traced here: 65.7 us
  Pallas kernels  63.7 us (97%)
  between operations  1.93 us (3%)
    pallas_call x1, Pallas kernels, body(): pl.pallas_call(kernel, out_shape=jax.ShapeDtypeStruct((3, images, width),...  60.9 us
    pallas_call x1, Pallas kernels, body(): pl.pallas_call(unstack, out_shape=(out, out, out), in_specs=[hbm], out_sp...  2.8 us

profile of v5, /device:TPU:1, one launch (start us, length us, event | category | flops | bytes accessed | tf_op | source)
XLA Modules:
  0.0 65.7 jit_solution(18151618221309959569)
XLA Ops:
  1.9 60.9 %shard_map.139.stacked_ref = f32[3,4,1152]{2,1,0:T(4,128)} custom-call(bf16[4,256,1152]{2,1,0:T(8,128)(2,1)} %patches_hbm.1, bf16[1152]{0:T(1024)(128)(2,1)} %norm_gain_hbm.1, bf16[1152,128]{1,0:T(8,128)(2,1)} %router_hbm.1, bf16[1,4304,1152]{2,1,0:T(8,128)(2,1)} %bitcast.1, bf16[1,4304,1152]{2,1,0:T(8,128)(2,1)} %out_hbm.1, bf16[1152]{0:T(1024)(128)(2,1)} %post_gain_hbm.1, ...), custom_call_target="tpu_custom_call" | custom-call | flops 12000000000 | bytes 40000000 | tf_op jit(solution)/shard_map/pallas_call | solution.py:352
  62.9 2.8 %shard_map.140 = (f32[4,1152]{1,0:T(4,128)}, f32[4,1152]{1,0:T(4,128)}, f32[4,1152]{1,0:T(4,128)}) custom-call(f32[3,4,1152]{2,1,0:T(4,128)} %shard_map.139.stacked_ref), custom_call_target="tpu_custom_call" | custom-call | tf_op jit(solution)/shard_map/pallas_call | solution.py:400
